TPU v7x, 32 devices: a whole 2x2x4 slice. The times are simulated.
32 devices in a mesh: tile: 4 (over z), eval: 8 (over y, x, core).
Axes of the slice: x: 2, y: 2, z: 4, core: 2. Of those that a mesh axis runs over, the one named last changes fastest.
Arguments:
- target_geom: float32 [6, 32, 1024], P(None, 'tile', 'eval'), may hold values from -1 to 1
- eta: float32 [32, 1024], P('tile', 'eval'), may hold values from -3 to 3
- phi: float32 [32, 1024], P('tile', 'eval'), may hold values from -3 to 3
- sources: float32 [4, 4, 4, 256], P('tile', None, None, 'eval')
- group_len: int32 [4, 8], replicated, may hold values from 1 to 32, 160 in all within a row
- owner: int32 [4], replicated, may hold values from 0 to 3, each once
Outputs:
- eta_next: float32 [32, 1024], P('tile', 'eval')
- phi_next: float32 [32, 1024], P('tile', 'eval')
- normal_velocity: float32 [32, 1024], P('tile', 'eval')
Inputs may be any that keep to these rules, and one draw needn't show every extreme that they name: owner holds distinct tile rows; round r's group is held by tile row owner[r]. `group_len`: each round has some column with all 32 slots live.
All inputs are finite; a program needn't handle non-finite values.
Results may differ from a plain program's by a relative error of at most 0.0001.
Values sent between devices are 32-bit elements; how exact they have to be, the bound alone decides.
A program may use at most 64 MiB of HBM per device.

v0:
```python
import jax
import jax.numpy as jnp
from jax import lax
from jax.sharding import PartitionSpec as P

ROUNDS = 4


EPS2 = 0.05


def spread(value, axis, source):
    kept = jnp.where(lax.axis_index(axis) == source, value, 0).astype(value.dtype)
    return lax.psum(kept, axis)


def with_halo(x, sides, width):
    for axis, dim in sides:
        peers, length = (lax.axis_size(axis), x.shape[dim])
        up = [(i, (i + 1) % peers) for i in range(peers - 1)]
        down = [(j, i) for i, j in up]
        last = lax.slice_in_dim(x, length - width, length, axis=dim)
        first = lax.slice_in_dim(x, 0, width, axis=dim)
        before = lax.ppermute(last, axis, up)
        after = lax.ppermute(first, axis, down)
        x = jnp.concatenate([before, x, after], axis=dim)
    return x


def kernel_sum(targ, src):
    dx = targ[0][None] - src[0][:, None, None]
    dy = targ[1][None] - src[1][:, None, None]
    dz = targ[2][None] - src[2][:, None, None]
    dist2 = dx * dx + dy * dy + dz * dz + EPS2
    numer = targ[3][None] * dx + targ[4][None] * dy + targ[5][None] * dz
    return jnp.sum(src[3][:, None, None] * numer / (dist2 * jnp.sqrt(dist2)), axis=0)


def all_rounds(targ, stacked):
    total = kernel_sum(targ, stacked[0])
    for step in range(1, stacked.shape[0]):
        total = total + kernel_sum(targ, stacked[step])
    return total


def tendency(ext):
    centre = ext[:, 1:-1, 1:-1]
    grad_x = (ext[:, 2:, 1:-1] - ext[:, :-2, 1:-1]) * 0.5
    grad_y = (ext[:, 1:-1, 2:] - ext[:, 1:-1, :-2]) * 0.5
    slope = 1.0 + grad_x[0] * grad_x[0] + grad_y[0] * grad_y[0]
    velocity = centre[2]
    eta_rate = velocity * slope - (grad_x[1] * grad_x[0] + grad_y[1] * grad_y[0])
    phi_rate = (
        -centre[0]
        - 0.5 * (grad_x[1] * grad_x[1] + grad_y[1] * grad_y[1])
        + 0.5 * velocity * velocity * slope
    )
    return jnp.stack([eta_rate, phi_rate])


def smooth(rim):
    centre = rim[:, 1:-1, 1:-1]
    return (
        4.0 * centre + rim[:, 2:, 1:-1] + rim[:, :-2, 1:-1] + rim[:, 1:-1, 2:] + rim[:, 1:-1, :-2]
    ) / 8.0


def mask_strength(block, group_len, step, column):
    width = block.shape[1]
    length = lax.dynamic_index_in_dim(group_len[step], column, 0, keepdims=False)
    live = (jnp.arange(width, dtype=jnp.int32) < length).astype(jnp.float32)
    return jnp.concatenate([block[:3], block[3:] * live[None]], axis=0)


def body(target_geom, eta, phi, sources, group_len, owner):
    column = lax.axis_index("eval")
    blocks = []
    for step in range(ROUNDS):
        own_block = mask_strength(sources[0, step], group_len, step, column)
        blocks.append(spread(own_block, "tile", owner[step]))
    stacked = jnp.stack(blocks)
    velocity = all_rounds(target_geom, lax.all_gather(stacked, "eval", axis=2, tiled=True))
    fields = jnp.stack([eta, phi, velocity])
    rows_here, cols_here = eta.shape
    ext = with_halo(fields, (("tile", 1), ("eval", 2)), 2)
    rates = tendency(ext)
    row_ids = lax.axis_index("tile") * rows_here + jnp.arange(rows_here + 2, dtype=jnp.int32) - 1
    col_ids = column * cols_here + jnp.arange(cols_here + 2, dtype=jnp.int32) - 1
    row_ok = (row_ids >= 0) & (row_ids < rows_here * lax.axis_size("tile"))
    col_ok = (col_ids >= 0) & (col_ids < cols_here * lax.axis_size("eval"))
    inside = (row_ok[:, None] & col_ok[None, :]).astype(jnp.float32)
    smoothed = smooth(rates * inside[None])
    return (eta + 0.5 * smoothed[0], phi + 0.5 * smoothed[1], velocity)


def solution(mesh):
    return jax.shard_map(
        body,
        mesh=mesh,
        in_specs=(
            P(None, "tile", "eval"),
            P("tile", "eval"),
            P("tile", "eval"),
            P("tile", None, None, "eval"),
            P(),
            P(),
        ),
        out_specs=(P("tile", "eval"), P("tile", "eval"), P("tile", "eval")),
        check_vma=False,
    )
```

profile of v0, /device:TPU:3, one launch (start us, length us, event | category | flops | bytes accessed | tf_op | source)
XLA Modules:
  0.0 70.5 jit_solution(11141763126147383826)
XLA Ops:
  0.6 0.0 copy-start.6
  0.6 0.0 copy-start.4
  0.7 0.7 copy-done.6
  1.3 0.0 copy-start.5
  1.3 0.7 copy-done.5
  2.0 0.7 fusion.49
  2.6 0.0 copy-done.4
  5.3 0.7 constant_dynamic-slice_fusion
  6.0 0.6 constant_dynamic-slice_fusion.2
  6.6 2.6 %compare_select_fusion.3 = (f32[1,32]{1,0:T(1,128)S(1)}, f32[1,32]{1,0:T(1,128)S(1)}, f32[1,32]{1,0:T(1,128)S(1)}, f32[1,32]{1,0:T(1,128)S(1)}) fusion(f32[1,4,4,32]{3,2,1,0:T(4,128)S(1)} %copy-done.4, s32[]{:T(128)} %bitcast.4, s32[]{:T(128)} %bitcast.14, s32[]{:T(128)} %bitcast.9, s32[]{:T(128)} %bitcast.19), kind=kLoop, calls=%fused_computation.141 | loop fusion | flops 256 | bytes 1040 | tf_op jit(solution)/shard_map/mul | solution.py:72
  9.3 10.1 %all-reduce = (f32[1,4,32]{2,1,0:T(4,128)S(1)}, f32[1,4,32]{2,1,0:T(4,128)S(1)}, f32[1,4,32]{2,1,0:T(4,128)S(1)}, f32[1,4,32]{2,1,0:T(4,128)S(1)}) all-reduce(f32[1,4,32]{2,1,0:T(4,128)S(1)} %fusion.46, f32[1,4,32]{2,1,0:T(4,128)S(1)} %fusion.45, f32[1,4,32]{2,1,0:T(4,128)S(1)} %fusion.44, ...), channel_id=1, replica_groups=mesh['tile'=4,'eval'=8] {'tile'}, use_global_device_ids=true, to_apply=%region_3.4 | all-reduce | flops 512 | bytes 4096 | tf_op jit(solution)/shard_map/psum | solution.py:14
  19.4 0.1 copy.11
  19.5 12.5 %all_gather.3 = f32[4,4,256]{1,0,2:T(4,128)S(1)} all-gather(f32[4,4,32]{1,0,2:T(4,128)S(1)} %copy.11), channel_id=1, replica_groups=mesh['tile'=4,'eval'=8] {'eval'}, dimensions={2}, use_global_device_ids=true | all-gather | bytes 18432 | tf_op jit(solution)/shard_map/all_gather | solution.py:82
  32.0 0.0 copy-start.3
  32.0 15.4 %slice_reduce_fusion.11 = (f32[256]{0:T(256)S(1)}, f32[256]{0:T(256)S(1)}, f32[256]{0:T(256)S(1)}, f32[256]{0:T(256)S(1)}, f32[256]{0:T(256)S(1)}, /*index=5*/f3...) fusion(f32[4,4,256]{1,0,2:T(4,128)S(1)} %all_gather.3), kind=kLoop, calls=%fused_computation.71 | loop fusion | bytes 32768 | tf_op jit(solution)/shard_map/slice | solution.py:36
  47.5 0.0 copy-done.3
  47.5 1.6 %fusion.7 = f32[8,128]{1,0:T(8,128)S(1)} fusion(f32[256]{0:T(256)S(1)} %get-tuple-element.15, f32[8,128]{1,0:T(8,128)S(1)} %get-tuple-element.34, f32[8,128]{1,0:T(8,128)S(1)} %get-tuple-element.35, f32[256]{0:T(256)S(1)} %get-tuple-element.16, f32[8,128]{1,0:T(8,128)S(1)} %get-tuple-element.31, f32[8,128]{1,0:T(8,128)S(1)} %get-tuple-element.32, ...), kind=kLoop, calls=%fused_computation.35 | loop fusion | flops 4717568 | bytes 32768 | tf_op jit(solution)/shard_map/reduce_sum | solution.py:36
  49.0 3.6 %fusion.15 = (f32[8,128]{1,0:T(8,128)S(1)}, f32[8,128]{1,0:T(8,128)S(1)}, f32[8,128]{1,0:T(8,128)S(1)}) fusion(f32[256]{0:T(256)S(1)} %get-tuple-element.12, f32[256]{0:T(256)S(1)} %get-tuple-element.13, f32[256]{0:T(256)S(1)} %get-tuple-element.14, f32[256]{0:T(256)S(1)} %get-tuple-element.3, f32[8,128]{1,0:T(8,128)S(1)} %get-tuple-element.34, ...), kind=kLoop, calls=%fused_computation.43 | loop fusion | flops 14152704 | bytes 49152 | tf_op jit(solution)/shard_map/reduce_sum | solution.py:36
  52.6 0.0 copy-start.2
  52.7 0.0 copy-start
  52.7 0.0 copy-start.1
  52.7 0.6 copy-done.2
  53.3 0.0 copy-done.1
  53.4 1.3 %collective-permute-start = (f32[3,2,128]{2,1,0:T(2,128)S(1)}, f32[3,2,128]{2,1,0:T(2,128)S(1)}, u32[]{:S(2)}, u32[]{:S(2)}) collective-permute-start(f32[3,2,128]{2,1,0:T(2,128)S(1)} %get-tuple-element.36), channel_id=1, source_target_pairs={{0,8},{8,16},{16,24},{1,9},{9,17},{17,25},{2,10},{10,18},{18,26},{... | collective-permute-start | bytes 9224 | tf_op jit(solution)/shard_map/ppermute | solution.py:24
  54.7 1.3 %collective-permute-start.1 = (f32[3,2,128]{2,1,0:T(2,128)S(1)}, f32[3,2,128]{2,1,0:T(2,128)S(1)}, u32[]{:S(2)}, u32[]{:S(2)}) collective-permute-start(f32[3,2,128]{2,1,0:T(2,128)S(1)} %get-tuple-element.37), channel_id=1, source_target_pairs={{8,0},{16,8},{24,16},{9,1},{17,9},{25,17},{10,2},{18,10},{26,18},{... | collective-permute-start | bytes 9224 | tf_op jit(solution)/shard_map/ppermute | solution.py:25
  56.0 0.0 collective-permute-done
  56.0 3.0 %collective-permute-done.1 = f32[3,2,128]{2,1,0:T(2,128)S(1)} collective-permute-done((f32[3,2,128]{2,1,0:T(2,128)S(1)}, f32[3,2,128]{2,1,0:T(2,128)S(1)}, u32[]{:S(2)}, u32[]{:S(2)}) %collective-permute-start.1) | collective-permute-done | bytes 3104 | tf_op jit(solution)/shard_map/ppermute | solution.py:25
  59.0 0.1 fusion.47
  59.1 4.3 %collective-permute-start.2 = (f32[3,12,2]{2,1,0:T(8,128)S(1)}, f32[3,12,2]{2,1,0:T(8,128)S(1)}, u32[]{:S(2)}, u32[]{:S(2)}) collective-permute-start(f32[3,12,2]{2,1,0:T(8,128)S(1)} %get-tuple-element.28), channel_id=1, source_target_pairs={{0,1},{1,2},{2,3},{3,4},{4,5},{5,6},{6,7},{8,9},{9,10},{10,11},{11... | collective-permute-start | bytes 872 | tf_op jit(solution)/shard_map/ppermute | solution.py:24
  63.4 1.9 %collective-permute-start.3 = (f32[3,12,2]{2,1,0:T(8,128)S(1)}, f32[3,12,2]{2,1,0:T(8,128)S(1)}, u32[]{:S(2)}, u32[]{:S(2)}) collective-permute-start(f32[3,12,2]{2,1,0:T(8,128)S(1)} %get-tuple-element.29), channel_id=1, source_target_pairs={{1,0},{2,1},{3,2},{4,3},{5,4},{6,5},{7,6},{9,8},{10,9},{11,10},{12... | collective-permute-start | bytes 872 | tf_op jit(solution)/shard_map/ppermute | solution.py:25
  65.3 0.1 and_convert_fusion
  65.4 0.0 collective-permute-done.2
  65.4 4.0 %collective-permute-done.3 = f32[3,12,2]{2,1,0:T(8,128)S(1)} collective-permute-done((f32[3,12,2]{2,1,0:T(8,128)S(1)}, f32[3,12,2]{2,1,0:T(8,128)S(1)}, u32[]{:S(2)}, u32[]{:S(2)}) %collective-permute-start.3) | collective-permute-done | bytes 320 | tf_op jit(solution)/shard_map/ppermute | solution.py:25
  69.4 0.1 pad_maximum_fusion.10
  69.5 0.1 fusion.34
  69.6 0.0 copy-done
  69.6 0.1 fusion.33
  69.7 0.1 add_subtract_fusion
  69.8 0.1 fusion.38
  69.9 0.6 fusion.40
  (14 shorter events, 0.1 us)
Async XLA Ops:
  0.6 0.7 copy-start.6
  0.6 2.0 %copy-start.4 = (f32[1,4,4,32]{3,2,1,0:T(4,128)S(1)}, f32[1,4,4,32]{3,2,1,0:T(4,128)}, u32[]{:S(2)}) copy-start(f32[1,4,4,32]{3,2,1,0:T(4,128)} %param.9) | copy-start | bytes 6148
  1.3 0.7 copy-start.5
  32.0 15.4 %copy-start.3 = (f32[6,8,128]{2,1,0:T(8,128)S(1)}, f32[6,8,128]{2,1,0:T(8,128)}, u32[]{:S(2)}) copy-start(f32[6,8,128]{2,1,0:T(8,128)} %param.6) | copy-start | bytes 73732
  52.6 0.7 copy-start.2
  52.7 17.0 %copy-start = (f32[8,128]{1,0:T(8,128)}, f32[8,128]{1,0:T(8,128)S(1)}, u32[]{:S(2)}) copy-start(f32[8,128]{1,0:T(8,128)S(1)} %add_add_fusion) | copy-start | bytes 12292
  52.7 0.7 copy-start.1
  53.4 2.6 %collective-permute-start = (f32[3,2,128]{2,1,0:T(2,128)S(1)}, f32[3,2,128]{2,1,0:T(2,128)S(1)}, u32[]{:S(2)}, u32[]{:S(2)}) collective-permute-start(f32[3,2,128]{2,1,0:T(2,128)S(1)} %get-tuple-element.36), channel_id=1, source_target_pairs={{0,8},{8,16},{16,24},{1,9},{9,17},{17,25},{2,10},{10,18},{18,26},{... | collective-permute-start | bytes 9224 | tf_op jit(solution)/shard_map/ppermute | solution.py:24
  54.7 4.3 %collective-permute-start.1 = (f32[3,2,128]{2,1,0:T(2,128)S(1)}, f32[3,2,128]{2,1,0:T(2,128)S(1)}, u32[]{:S(2)}, u32[]{:S(2)}) collective-permute-start(f32[3,2,128]{2,1,0:T(2,128)S(1)} %get-tuple-element.37), channel_id=1, source_target_pairs={{8,0},{16,8},{24,16},{9,1},{17,9},{25,17},{10,2},{18,10},{26,18},{... | collective-permute-start | bytes 9224 | tf_op jit(solution)/shard_map/ppermute | solution.py:25
  59.1 6.3 %collective-permute-start.2 = (f32[3,12,2]{2,1,0:T(8,128)S(1)}, f32[3,12,2]{2,1,0:T(8,128)S(1)}, u32[]{:S(2)}, u32[]{:S(2)}) collective-permute-start(f32[3,12,2]{2,1,0:T(8,128)S(1)} %get-tuple-element.28), channel_id=1, source_target_pairs={{0,1},{1,2},{2,3},{3,4},{4,5},{5,6},{6,7},{8,9},{9,10},{10,11},{11... | collective-permute-start | bytes 872 | tf_op jit(solution)/shard_map/ppermute | solution.py:24
  63.4 6.0 %collective-permute-start.3 = (f32[3,12,2]{2,1,0:T(8,128)S(1)}, f32[3,12,2]{2,1,0:T(8,128)S(1)}, u32[]{:S(2)}, u32[]{:S(2)}) collective-permute-start(f32[3,12,2]{2,1,0:T(8,128)S(1)} %get-tuple-element.29), channel_id=1, source_target_pairs={{1,0},{2,1},{3,2},{4,3},{5,4},{6,5},{7,6},{9,8},{10,9},{11,10},{12... | collective-permute-start | bytes 872 | tf_op jit(solution)/shard_map/ppermute | solution.py:25
where the time goes:
time: 70.9 us; the launch traced here: 70.5 us
  blocking collectives  22.6 us (32%)
  local copies, waits for them, and re-layouts  19.6 us (28%)
  other arithmetic  9.01 us (13%)
  starting transfers between devices  8.76 us (12%)
  waiting for transfers between devices  7.04 us (10%)
  between operations  3.52 us (5%)
    slice x1, local copies, waits for them, and re-layouts, kernel_sum(): src[3][:, None, None] * numer / (dist2 * jnp.sqrt(dist2))  15.4 us
    all_gather x1, blocking collectives, body(): lax.all_gather(stacked, 'eval', axis=2, tiled=True)  12.5 us
    psum x1, blocking collectives, spread(): return lax.psum(kept, axis)  10.1 us
    ppermute x2, waiting for transfers between devices, with_halo(): after = lax.ppermute(first, axis, down)  7.03 us
    ppermute x2, starting transfers between devices, with_halo(): before = lax.ppermute(last, axis, up)  5.55 us
    reduce_sum x2, other arithmetic, kernel_sum(): jnp.sum(src[3][:, None, None] * numer / (dist2 * jnp.sqrt(dist2)), axis=0)  5.15 us
    ppermute x2, starting transfers between devices, with_halo(): after = lax.ppermute(first, axis, down)  3.21 us
    mul x1, other arithmetic, mask_strength(): return jnp.concatenate([block[:3], block[3:] * live[None]], axis=0)  2.63 us
  transfers between devices with their start and end apart: 4, of which 2 were waited for; matrix products, arithmetic and copies ran while one was open for 0% of the time, Pallas kernels for 0%

commit v1 on v0

v1 whole, which is shorter than its diff:
```python
import functools

import jax
import jax.numpy as jnp
from jax import lax
from jax.experimental import pallas as pl
from jax.experimental.pallas import tpu as pltpu
from jax.sharding import PartitionSpec as P

ROUNDS = 4
EPS2 = 0.05
HALF = 24
FEATS = 2 * HALF
MESH = pl.DeviceIdType.MESH
F32 = jnp.float32
BF16 = jnp.bfloat16


def split3(v):
    hi = v.astype(BF16).astype(F32)
    rest = v - hi
    mid = rest.astype(BF16).astype(F32)
    low = (rest - mid).astype(BF16).astype(F32)
    return hi, mid, low


def left_six(v):
    a, b, c = split3(v)
    return [a, a, b, a, c, b]


def right_six(v):
    a, b, c = split3(v)
    return [a, b, a, c, a, b]


def target_features(geom):
    x, n = geom[:3], geom[3:]
    one = jnp.ones_like(x[0])
    rows = []
    for c in range(3):
        rows += right_six(x[c])
    rows += list(split3(x[0] * x[0] + x[1] * x[1] + x[2] * x[2] + EPS2))
    rows += [one, one, one]
    for c in range(3):
        rows += right_six(n[c])
    rows += right_six(n[0] * x[0] + n[1] * x[1] + n[2] * x[2])
    return rows


def source_features(y, q):
    one = jnp.ones_like(q)
    rows = []
    for c in range(3):
        rows += left_six(-2.0 * y[c])
    rows += [one, one, one]
    rows += list(split3(y[0] * y[0] + y[1] * y[1] + y[2] * y[2]))
    for c in range(3):
        rows += left_six(-q * y[c])
    rows += left_six(q)
    return rows


def kernel(
    tiles, evals,
    geom, eta, phi, src, glen, owner, out,
    row_out, rows_top, rows_bot, cols_out,
    got, halo_rows, halo_diag, halo_cols,
    tfeat, sfeat, lhs, ext,
    send_src, recv_src, send_halo, recv_halo,
):
    ti, ev = lax.axis_index("tile"), lax.axis_index("eval")
    peers = tiles * evals
    me = ti * evals + ev
    up, down = lax.rem(ti + tiles - 1, tiles), lax.rem(ti + 1, tiles)
    left, right = lax.rem(ev + evals - 1, evals), lax.rem(ev + 1, evals)

    barrier = pltpu.get_barrier_semaphore()

    def greet(k, carry):
        other = lax.rem(me + k, peers)
        pl.semaphore_signal(
            barrier, inc=1,
            device_id=(lax.div(other, evals), lax.rem(other, evals)), device_id_type=MESH,
        )
        return carry

    lax.fori_loop(1, peers, greet, 0)

    width = src.shape[3]
    slot = lax.broadcasted_iota(jnp.int32, (1, width), 1)
    block = jnp.zeros((4, width), F32)
    for r in range(ROUNDS):
        mine = owner[r] == ti
        live = (slot < glen[r, ev]).astype(F32)
        this = src[0, r]
        this = jnp.concatenate([jnp.clip(this[:3], -1e18, 1e18), this[3:] * live], axis=0)
        block = jnp.where(mine, this, block)
    row = jnp.concatenate([block[f:f + 1] for f in range(4)], axis=1)
    row_out[0] = row
    got[me] = row

    height, lanes = eta.shape
    e, p = eta[...], phi[...]
    g = [geom[f] for f in range(6)]
    last = height - 1
    pad = jnp.zeros((6, lanes), F32)
    rows_top[...] = jnp.concatenate(
        [e[0:1], p[0:1], e[1:2], p[1:2]] + [v[0:1] for v in g] + [pad], axis=0)
    rows_bot[...] = jnp.concatenate(
        [e[last:], p[last:], e[last - 1:last], p[last - 1:last]] + [v[last:] for v in g] + [pad],
        axis=0)
    lane = lax.broadcasted_iota(jnp.int32, (height, lanes), 1)
    end = lanes - 1
    columns = [e[:, 0:1], p[:, 0:1], e[:, 1:2], p[:, 1:2]] + [v[:, 0:1] for v in g]
    columns2 = [e[:, end:], p[:, end:], e[:, end - 1:end], p[:, end - 1:end]] + [v[:, end:] for v in g]
    cols = jnp.zeros((height, lanes), F32)
    for k, v in enumerate(columns):
        cols = jnp.where(lane == k, v, cols)
    for k, v in enumerate(columns2):
        cols = jnp.where(lane == 16 + k, v, cols)
    cols_out[...] = cols

    pl.semaphore_wait(barrier, peers - 1)

    def send(k, carry):
        other = lax.rem(me + k, peers)
        pltpu.make_async_remote_copy(
            src_ref=row_out.at[0], dst_ref=got.at[me], send_sem=send_src, recv_sem=recv_src,
            device_id=(lax.div(other, evals), lax.rem(other, evals)), device_id_type=MESH,
        ).start()
        return carry

    lax.fori_loop(1, peers, send, 0)
    first = pl.ds(0, 8)
    plan = [
        (rows_top, halo_rows.at[1], (up, ev)),
        (rows_bot, halo_rows.at[0], (down, ev)),
        (cols_out, halo_cols.at[1], (ti, left)),
        (cols_out, halo_cols.at[0], (ti, right)),
        (rows_top.at[first], halo_diag.at[3], (up, left)),
        (rows_top.at[first], halo_diag.at[2], (up, right)),
        (rows_bot.at[first], halo_diag.at[1], (down, left)),
        (rows_bot.at[first], halo_diag.at[0], (down, right)),
    ]
    copies = []
    for k, (a, b, where) in enumerate(plan):
        copy = pltpu.make_async_remote_copy(
            src_ref=a, dst_ref=b, send_sem=send_halo.at[k], recv_sem=recv_halo.at[k],
            device_id=where, device_id_type=MESH)
        copy.start()
        copies.append(copy)

    for k, v in enumerate(target_features(g)):
        tfeat[0:height, k, :] = v
    ext[...] = jnp.zeros_like(ext)
    for f, v in enumerate((e, p)):
        ext[f, 8:16, 0:lanes] = v

    for copy in copies:
        copy.wait()

    has_up, has_down = ti > 0, ti < tiles - 1
    has_left, has_right = ev > 0, ev < evals - 1
    above, below = halo_rows[0], halo_rows[1]
    near = [jnp.concatenate([above[4 + f:5 + f], below[4 + f:5 + f]], axis=0) for f in range(6)]
    for k, v in enumerate(target_features(near)):
        tfeat[height:height + 2, k, :] = v
    cl, cr = halo_cols[0], halo_cols[1]
    for f in range(2):
        ext[f, 7:8, 0:lanes] = jnp.where(has_up, above[f:f + 1], 0.0)
        ext[f, 6:7, 0:lanes] = jnp.where(has_up, above[2 + f:3 + f], 0.0)
        ext[f, 16:17, 0:lanes] = jnp.where(has_down, below[f:f + 1], 0.0)
        ext[f, 17:18, 0:lanes] = jnp.where(has_down, below[2 + f:3 + f], 0.0)
        lane1 = lane[0:1]

        def side(lf, rt):
            at = lane if lf[0].shape[0] > 1 else lane1
            v = jnp.zeros(at.shape, F32)
            for k, c in enumerate(rt):
                v = jnp.where((at == k) & has_right, c, v)
            for k, c in enumerate(lf):
                v = jnp.where((at == end - k) & has_left, c, v)
            return v

        ext[f, 8:16, lanes:] = side(
            [cl[:, 16 + f:17 + f], cl[:, 18 + f:19 + f]], [cr[:, f:f + 1], cr[:, 2 + f:3 + f]])
        ext[f, 7:8, lanes:] = jnp.where(
            has_up, side([halo_diag[0, f:f + 1, end:]], [halo_diag[1, f:f + 1, 0:1]]), 0.0)
        ext[f, 16:17, lanes:] = jnp.where(
            has_down, side([halo_diag[2, f:f + 1, end:]], [halo_diag[3, f:f + 1, 0:1]]), 0.0)

    others = got.at[pl.ds(0, peers - 1)]
    pltpu.make_async_copy(others, others, recv_src).wait()
    pltpu.make_async_copy(others, others, send_src).wait()

    table = got[:, 0, :]
    if tiles > ROUNDS:
        picked = []
        for r in range(ROUNDS):
            v = jnp.zeros((evals, 4 * width), F32)
            for t in range(tiles):
                v = jnp.where(owner[r] == t, table[t * evals:(t + 1) * evals], v)
            picked.append(v)
        table = jnp.concatenate(picked, axis=0)
    chunks = table.shape[0] // 4
    group = lax.div(lax.broadcasted_iota(jnp.int32, (chunks, 4 * width), 1), width)
    parts = [table[b * chunks:(b + 1) * chunks] for b in range(4)]
    s = []
    for f in range(4):
        v = parts[f]
        for b in range(4):
            if b != f:
                v = jnp.where(group == b, pltpu.roll(parts[b], ((b - f) % 4) * width, 1), v)
        s.append(v)
    y, q = s[:3], s[3]
    for k, v in enumerate(source_features(y, q)):
        sfeat[:, k, :] = v
    wide = 4 * width
    feat = lax.broadcasted_iota(jnp.int32, (wide, FEATS), 1)

    def turn(a, carry):
        t = sfeat[a].T
        lhs[a, 0:wide, :] = jnp.where(feat < HALF, t, 0.0).astype(BF16)
        lhs[a, wide:, :] = jnp.where(feat >= HALF, t, 0.0).astype(BF16)
        return carry

    lax.fori_loop(0, chunks, turn, 0, unroll=min(chunks, 8))

    for n in range(height // 2 + 1):
        rhs = jnp.concatenate([tfeat[2 * n], tfeat[2 * n + 1]], axis=1).astype(BF16)

        def add(a, acc):
            both = jnp.dot(lhs[a], rhs, preferred_element_type=F32)
            dist2, numer = both[:wide], both[wide:]
            r = lax.rsqrt(dist2)
            term = (numer * r) * (r * r)
            return acc + jnp.sum(term.reshape(wide // 8, 8, 2 * lanes), axis=0)

        acc = lax.fori_loop(0, chunks, add, jnp.zeros((8, 2 * lanes), F32), unroll=min(chunks, 8))
        w = jnp.sum(acc, axis=0, keepdims=True)
        if n < height // 2:
            ext[2, 8 + 2 * n:9 + 2 * n, 0:lanes] = w[:, :lanes]
            ext[2, 9 + 2 * n:10 + 2 * n, 0:lanes] = w[:, lanes:]
        else:
            ext[2, 7:8, 0:lanes] = jnp.where(has_up, w[:, :lanes], 0.0)
            ext[2, 16:17, 0:lanes] = jnp.where(has_down, w[:, lanes:], 0.0)

    total = [jnp.zeros((height, wide), F32) for _ in range(2)]
    sides = [[c[:, k:k + 1] for k in range(o, o + 6)] for c, o in ((cl, 20), (cr, 4))]
    sides = [[jnp.broadcast_to(v, (height, wide)) for v in one] for one in sides]
    for a in range(chunks):
        ya = [jnp.broadcast_to(v[a:a + 1], (height, wide)) for v in s]
        for k, t in enumerate(sides):
            d = [t[c] - ya[c] for c in range(3)]
            r = lax.rsqrt(d[0] * d[0] + d[1] * d[1] + d[2] * d[2] + EPS2)
            numer = t[3] * d[0] + t[4] * d[1] + t[5] * d[2]
            total[k] = total[k] + (ya[3] * numer * r) * (r * r)
    wl = jnp.sum(total[0], axis=1, keepdims=True)
    wr = jnp.sum(total[1], axis=1, keepdims=True)
    halo = jnp.where((lane == 0) & has_right, wr, 0.0)
    ext[2, 8:16, lanes:] = jnp.where((lane == end) & has_left, wl, halo)

    span = (24, 2 * lanes)
    ee, pp, ww = ext[0], ext[1], ext[2]
    hi = lambda v, axis: pltpu.roll(v, span[axis] - 1, axis)
    lo = lambda v, axis: pltpu.roll(v, 1, axis)
    grad = lambda v, axis: (hi(v, axis) - lo(v, axis)) * 0.5
    ex, ey, px, py = grad(ee, 0), grad(ee, 1), grad(pp, 0), grad(pp, 1)
    slope = 1.0 + ex * ex + ey * ey
    erate = ww * slope - (px * ex + py * ey)
    prate = -ee - 0.5 * (px * px + py * py) + 0.5 * ww * ww * slope
    ri = lax.broadcasted_iota(jnp.int32, span, 0)
    ci = lax.broadcasted_iota(jnp.int32, span, 1)
    inside = ((ri >= 8) | has_up) & ((ri < 16) | has_down)
    inside = inside & ((ci < lanes) | ((ci < lanes + lanes // 2) & has_right)
                       | ((ci >= lanes + lanes // 2) & has_left))

    def smooth(v):
        v = jnp.where(inside, v, 0.0)
        v = (4.0 * v + hi(v, 0) + lo(v, 0) + hi(v, 1) + lo(v, 1)) * 0.125
        return v[8:16, :lanes]

    out[0] = e + 0.5 * smooth(erate)
    out[1] = p + 0.5 * smooth(prate)
    out[2] = ww[8:16, :lanes]


def body(tiles, evals, target_geom, eta, phi, sources, group_len, owner):
    height, lanes = eta.shape
    width = sources.shape[3]
    chunks = ROUNDS * evals // 4
    vmem = pl.BlockSpec(memory_space=pltpu.VMEM)
    smem = pl.BlockSpec(memory_space=pltpu.SMEM)
    out = pl.pallas_call(
        functools.partial(kernel, tiles, evals),
        out_shape=jax.ShapeDtypeStruct((3, height, lanes), F32),
        in_specs=[vmem] * 4 + [smem] * 2,
        out_specs=vmem,
        scratch_shapes=[
            pltpu.VMEM((1, 1, 4 * width), F32),
            pltpu.VMEM((16, lanes), F32),
            pltpu.VMEM((16, lanes), F32),
            pltpu.VMEM((height, lanes), F32),
            pltpu.VMEM((tiles * evals, 1, 4 * width), F32),
            pltpu.VMEM((2, 16, lanes), F32),
            pltpu.VMEM((4, 8, lanes), F32),
            pltpu.VMEM((2, height, lanes), F32),
            pltpu.VMEM((height + 2, FEATS, lanes), F32),
            pltpu.VMEM((chunks, FEATS, 4 * width), F32),
            pltpu.VMEM((chunks, 8 * width, FEATS), BF16),
            pltpu.VMEM((3, 24, 2 * lanes), F32),
            pltpu.SemaphoreType.DMA,
            pltpu.SemaphoreType.DMA,
            pltpu.SemaphoreType.DMA((8,)),
            pltpu.SemaphoreType.DMA((8,)),
        ],
        compiler_params=pltpu.CompilerParams(
            collective_id=0, has_side_effects=True, vmem_limit_bytes=48 * 1024 * 1024),
    )(target_geom, eta, phi, sources, group_len, owner)
    return out[0], out[1], out[2]


def solution(mesh):
    return jax.shard_map(
        functools.partial(body, mesh.shape["tile"], mesh.shape["eval"]),
        mesh=mesh,
        in_specs=(
            P(None, "tile", "eval"),
            P("tile", "eval"),
            P("tile", "eval"),
            P("tile", None, None, "eval"),
            P(),
            P(),
        ),
        out_specs=(P("tile", "eval"), P("tile", "eval"), P("tile", "eval")),
        check_vma=False,
    )
```

time: 70.9 us -> 18 us (0.25)
  the two profiles are of different devices: /device:TPU:3 before, /device:TPU:0 now
where the time goes in v1:
time: 18 us; the launch traced here: 17.7 us
  Pallas kernels  12.3 us (68%)
  local copies, waits for them, and re-layouts  4.74 us (26%)
  between operations  0.65 us (4%)
    pallas_call x1, Pallas kernels, body(): pl.pallas_call(functools.partial(kernel, tiles, evals), out_shape=jax.Sha...  12.3 us
    unnamed x12, local copies, waits for them, and re-layouts  4.14 us
    squeeze x1, local copies, waits for them, and re-layouts, body(): return (out[0], out[1], out[2])  0.6 us

profile of v1, /device:TPU:0, one launch (start us, length us, event | category | flops | bytes accessed | tf_op | source)
XLA Modules:
  0.0 17.7 jit_solution(2361912322757134772)
XLA Ops:
  0.6 0.0 copy-start
  0.6 0.7 %copy-done = f32[6,8,128]{2,1,0:T(8,128)S(1)} copy-done((f32[6,8,128]{2,1,0:T(8,128)S(1)}, f32[6,8,128]{2,1,0:T(8,128)}, u32[]{:S(2)}) %copy-start) | copy-done | bytes 24600
  1.4 0.0 copy-start.1
  1.4 0.7 %copy-done.1 = f32[1,4,4,32]{3,2,1,0:T(4,128)S(1)} copy-done((f32[1,4,4,32]{3,2,1,0:T(4,128)S(1)}, f32[1,4,4,32]{3,2,1,0:T(4,128)}, u32[]{:S(2)}) %copy-start.1) | copy-done | bytes 2072
  2.1 0.0 copy-start.2
  2.1 0.7 %copy-done.2 = f32[8,128]{1,0:T(8,128)S(1)} copy-done((f32[8,128]{1,0:T(8,128)S(1)}, f32[8,128]{1,0:T(8,128)}, u32[]{:S(2)}) %copy-start.2) | copy-done | bytes 4120
  2.8 0.0 copy-start.3
  2.8 0.7 %copy-done.3 = f32[8,128]{1,0:T(8,128)S(1)} copy-done((f32[8,128]{1,0:T(8,128)S(1)}, f32[8,128]{1,0:T(8,128)}, u32[]{:S(2)}) %copy-start.3) | copy-done | bytes 4120
  3.4 0.0 copy-start.4
  3.4 0.7 %copy-done.4 = s32[4,8]{1,0:T(4,128)S(1)} copy-done((s32[4,8]{1,0:T(4,128)S(1)}, s32[4,8]{1,0:T(4,128)}, u32[]{:S(2)}) %copy-start.4) | copy-done | bytes 152
  4.1 0.0 copy-start.5
  4.1 0.7 %copy-done.5 = s32[4]{0:T(128)S(1)} copy-done((s32[4]{0:T(128)S(1)}, s32[4]{0:T(128)}, u32[]{:S(2)}) %copy-start.5) | copy-done | bytes 40
  4.8 12.3 %shard_map.85 = f32[3,8,128]{2,1,0:T(8,128)S(1)} custom-call(f32[6,8,128]{2,1,0:T(8,128)S(1)} %copy-done, f32[8,128]{1,0:T(8,128)S(1)} %copy-done.2, f32[8,128]{1,0:T(8,128)S(1)} %copy-done.3, f32[1,4,4,32]{3,2,1,0:T(4,128)S(1)} %copy-done.1, s32[4,8]{1,0:T(4,128)S(1)} %copy-done.4, s32[4]{0:T(128)S(1)} %copy-done.5), custom_call_target="tpu_custom_call" | custom-call | tf_op jit(solution)/shard_map/pallas_call | solution.py:295
  17.1 0.6 %slice_bitcast_fusion = (f32[8,128]{1,0:T(8,128)}, f32[8,128]{1,0:T(8,128)}, f32[8,128]{1,0:T(8,128)}) fusion(f32[3,8,128]{2,1,0:T(8,128)S(1)} %shard_map.85), kind=kLoop, calls=%fused_computation | loop fusion | bytes 24576 | tf_op jit(solution)/shard_map/squeeze | solution.py:321
Async XLA Ops:
  0.6 0.7 %copy-start = (f32[6,8,128]{2,1,0:T(8,128)S(1)}, f32[6,8,128]{2,1,0:T(8,128)}, u32[]{:S(2)}) copy-start(f32[6,8,128]{2,1,0:T(8,128)} %geom.1) | copy-start | bytes 73732
  1.4 0.7 %copy-start.1 = (f32[1,4,4,32]{3,2,1,0:T(4,128)S(1)}, f32[1,4,4,32]{3,2,1,0:T(4,128)}, u32[]{:S(2)}) copy-start(f32[1,4,4,32]{3,2,1,0:T(4,128)} %src.1) | copy-start | bytes 6148
  2.1 0.7 %copy-start.2 = (f32[8,128]{1,0:T(8,128)S(1)}, f32[8,128]{1,0:T(8,128)}, u32[]{:S(2)}) copy-start(f32[8,128]{1,0:T(8,128)} %eta.1) | copy-start | bytes 12292
  2.8 0.7 %copy-start.3 = (f32[8,128]{1,0:T(8,128)S(1)}, f32[8,128]{1,0:T(8,128)}, u32[]{:S(2)}) copy-start(f32[8,128]{1,0:T(8,128)} %phi.1) | copy-start | bytes 12292
  3.4 0.7 %copy-start.4 = (s32[4,8]{1,0:T(4,128)S(1)}, s32[4,8]{1,0:T(4,128)}, u32[]{:S(2)}) copy-start(s32[4,8]{1,0:T(4,128)} %glen.1) | copy-start | bytes 388
  4.1 0.7 %copy-start.5 = (s32[4]{0:T(128)S(1)}, s32[4]{0:T(128)}, u32[]{:S(2)}) copy-start(s32[4]{0:T(128)} %owner.1) | copy-start | bytes 52

commit v2 on v1

--- a/solution.py
+++ b/solution.py
@@ -63,12 +63,17 @@
 
 def kernel(
     tiles, evals,
-    geom, eta, phi, src, glen, owner, out,
-    row_out, rows_top, rows_bot, cols_out,
+    geom_in, eta_in, phi_in, src_in, glen_in, owner_in, out,
+    geom, eta, phi, src, glen, owner, row_out, rows_top, rows_bot, cols_out,
     got, halo_rows, halo_diag, halo_cols,
     tfeat, sfeat, lhs, ext,
-    send_src, recv_src, send_halo, recv_halo,
+    load, send_src, recv_src, send_halo, recv_halo,
 ):
+    pairs = ((src_in, src), (glen_in, glen), (owner_in, owner),
+             (geom_in, geom), (eta_in, eta), (phi_in, phi))
+    loads = [pltpu.make_async_copy(a, b, load.at[k]) for k, (a, b) in enumerate(pairs)]
+    for copy in loads:
+        copy.start()
     ti, ev = lax.axis_index("tile"), lax.axis_index("eval")
     peers = tiles * evals
     me = ti * evals + ev
@@ -87,6 +92,8 @@
 
     lax.fori_loop(1, peers, greet, 0)
 
+    for copy in loads[:3]:
+        copy.wait()
     width = src.shape[3]
     slot = lax.broadcasted_iota(jnp.int32, (1, width), 1)
     block = jnp.zeros((4, width), F32)
@@ -100,6 +107,8 @@
     row_out[0] = row
     got[me] = row
 
+    for copy in loads[3:]:
+        copy.wait()
     height, lanes = eta.shape
     e, p = eta[...], phi[...]
     g = [geom[f] for f in range(6)]
@@ -156,39 +165,6 @@
     ext[...] = jnp.zeros_like(ext)
     for f, v in enumerate((e, p)):
         ext[f, 8:16, 0:lanes] = v
-
-    for copy in copies:
-        copy.wait()
-
-    has_up, has_down = ti > 0, ti < tiles - 1
-    has_left, has_right = ev > 0, ev < evals - 1
-    above, below = halo_rows[0], halo_rows[1]
-    near = [jnp.concatenate([above[4 + f:5 + f], below[4 + f:5 + f]], axis=0) for f in range(6)]
-    for k, v in enumerate(target_features(near)):
-        tfeat[height:height + 2, k, :] = v
-    cl, cr = halo_cols[0], halo_cols[1]
-    for f in range(2):
-        ext[f, 7:8, 0:lanes] = jnp.where(has_up, above[f:f + 1], 0.0)
-        ext[f, 6:7, 0:lanes] = jnp.where(has_up, above[2 + f:3 + f], 0.0)
-        ext[f, 16:17, 0:lanes] = jnp.where(has_down, below[f:f + 1], 0.0)
-        ext[f, 17:18, 0:lanes] = jnp.where(has_down, below[2 + f:3 + f], 0.0)
-        lane1 = lane[0:1]
-
-        def side(lf, rt):
-            at = lane if lf[0].shape[0] > 1 else lane1
-            v = jnp.zeros(at.shape, F32)
-            for k, c in enumerate(rt):
-                v = jnp.where((at == k) & has_right, c, v)
-            for k, c in enumerate(lf):
-                v = jnp.where((at == end - k) & has_left, c, v)
-            return v
-
-        ext[f, 8:16, lanes:] = side(
-            [cl[:, 16 + f:17 + f], cl[:, 18 + f:19 + f]], [cr[:, f:f + 1], cr[:, 2 + f:3 + f]])
-        ext[f, 7:8, lanes:] = jnp.where(
-            has_up, side([halo_diag[0, f:f + 1, end:]], [halo_diag[1, f:f + 1, 0:1]]), 0.0)
-        ext[f, 16:17, lanes:] = jnp.where(
-            has_down, side([halo_diag[2, f:f + 1, end:]], [halo_diag[3, f:f + 1, 0:1]]), 0.0)
 
     others = got.at[pl.ds(0, peers - 1)]
     pltpu.make_async_copy(others, others, recv_src).wait()
@@ -227,7 +203,7 @@
 
     lax.fori_loop(0, chunks, turn, 0, unroll=min(chunks, 8))
 
-    for n in range(height // 2 + 1):
+    def velocity(n):
         rhs = jnp.concatenate([tfeat[2 * n], tfeat[2 * n + 1]], axis=1).astype(BF16)
 
         def add(a, acc):
@@ -238,13 +214,49 @@
             return acc + jnp.sum(term.reshape(wide // 8, 8, 2 * lanes), axis=0)
 
         acc = lax.fori_loop(0, chunks, add, jnp.zeros((8, 2 * lanes), F32), unroll=min(chunks, 8))
-        w = jnp.sum(acc, axis=0, keepdims=True)
-        if n < height // 2:
-            ext[2, 8 + 2 * n:9 + 2 * n, 0:lanes] = w[:, :lanes]
-            ext[2, 9 + 2 * n:10 + 2 * n, 0:lanes] = w[:, lanes:]
-        else:
-            ext[2, 7:8, 0:lanes] = jnp.where(has_up, w[:, :lanes], 0.0)
-            ext[2, 16:17, 0:lanes] = jnp.where(has_down, w[:, lanes:], 0.0)
+        return jnp.sum(acc, axis=0, keepdims=True)
+
+    for n in range(height // 2):
+        w = velocity(n)
+        ext[2, 8 + 2 * n:9 + 2 * n, 0:lanes] = w[:, :lanes]
+        ext[2, 9 + 2 * n:10 + 2 * n, 0:lanes] = w[:, lanes:]
+
+    has_up, has_down = ti > 0, ti < tiles - 1
+    has_left, has_right = ev > 0, ev < evals - 1
+    for copy in copies:
+        copy.wait()
+
+    above, below = halo_rows[0], halo_rows[1]
+    near = [jnp.concatenate([above[4 + f:5 + f], below[4 + f:5 + f]], axis=0) for f in range(6)]
+    for k, v in enumerate(target_features(near)):
+        tfeat[height:height + 2, k, :] = v
+    cl, cr = halo_cols[0], halo_cols[1]
+    for f in range(2):
+        ext[f, 7:8, 0:lanes] = jnp.where(has_up, above[f:f + 1], 0.0)
+        ext[f, 6:7, 0:lanes] = jnp.where(has_up, above[2 + f:3 + f], 0.0)
+        ext[f, 16:17, 0:lanes] = jnp.where(has_down, below[f:f + 1], 0.0)
+        ext[f, 17:18, 0:lanes] = jnp.where(has_down, below[2 + f:3 + f], 0.0)
+        lane1 = lane[0:1]
+
+        def side(lf, rt):
+            at = lane if lf[0].shape[0] > 1 else lane1
+            v = jnp.zeros(at.shape, F32)
+            for k, c in enumerate(rt):
+                v = jnp.where((at == k) & has_right, c, v)
+            for k, c in enumerate(lf):
+                v = jnp.where((at == end - k) & has_left, c, v)
+            return v
+
+        ext[f, 8:16, lanes:] = side(
+            [cl[:, 16 + f:17 + f], cl[:, 18 + f:19 + f]], [cr[:, f:f + 1], cr[:, 2 + f:3 + f]])
+        ext[f, 7:8, lanes:] = jnp.where(
+            has_up, side([halo_diag[0, f:f + 1, end:]], [halo_diag[1, f:f + 1, 0:1]]), 0.0)
+        ext[f, 16:17, lanes:] = jnp.where(
+            has_down, side([halo_diag[2, f:f + 1, end:]], [halo_diag[3, f:f + 1, 0:1]]), 0.0)
+
+    w = velocity(height // 2)
+    ext[2, 7:8, 0:lanes] = jnp.where(has_up, w[:, :lanes], 0.0)
+    ext[2, 16:17, 0:lanes] = jnp.where(has_down, w[:, lanes:], 0.0)
 
     total = [jnp.zeros((height, wide), F32) for _ in range(2)]
     sides = [[c[:, k:k + 1] for k in range(o, o + 6)] for c, o in ((cl, 20), (cr, 4))]
@@ -291,13 +303,19 @@
     width = sources.shape[3]
     chunks = ROUNDS * evals // 4
     vmem = pl.BlockSpec(memory_space=pltpu.VMEM)
-    smem = pl.BlockSpec(memory_space=pltpu.SMEM)
+    hbm = pl.BlockSpec(memory_space=pltpu.HBM)
     out = pl.pallas_call(
         functools.partial(kernel, tiles, evals),
         out_shape=jax.ShapeDtypeStruct((3, height, lanes), F32),
-        in_specs=[vmem] * 4 + [smem] * 2,
+        in_specs=[hbm] * 6,
         out_specs=vmem,
         scratch_shapes=[
+            pltpu.VMEM(target_geom.shape, F32),
+            pltpu.VMEM(eta.shape, F32),
+            pltpu.VMEM(phi.shape, F32),
+            pltpu.VMEM(sources.shape, F32),
+            pltpu.SMEM(group_len.shape, jnp.int32),
+            pltpu.SMEM(owner.shape, jnp.int32),
             pltpu.VMEM((1, 1, 4 * width), F32),
             pltpu.VMEM((16, lanes), F32),
             pltpu.VMEM((16, lanes), F32),
@@ -310,13 +328,14 @@
             pltpu.VMEM((chunks, FEATS, 4 * width), F32),
             pltpu.VMEM((chunks, 8 * width, FEATS), BF16),
             pltpu.VMEM((3, 24, 2 * lanes), F32),
+            pltpu.SemaphoreType.DMA((6,)),
             pltpu.SemaphoreType.DMA,
             pltpu.SemaphoreType.DMA,
             pltpu.SemaphoreType.DMA((8,)),
             pltpu.SemaphoreType.DMA((8,)),
         ],
         compiler_params=pltpu.CompilerParams(
-            collective_id=0, has_side_effects=True, vmem_limit_bytes=48 * 1024 * 1024),
+            collective_id=0, has_side_effects=True),
     )(target_geom, eta, phi, sources, group_len, owner)
     return out[0], out[1], out[2]
 

time: 18 us -> 14.5 us (0.81)
  local copies, waits for them, and re-layouts: 4.74 us -> 1.29 us
    unnamed x12 -> x0, local copies, waits for them, and re-layouts: 4.14 us -> none
    squeeze x1, local copies, waits for them, and re-layouts: 0.6 us -> 1.29 us  [body(): return (out[0], out[1], out[2])]
where the time goes in v2:
time: 14.5 us; the launch traced here: 14.3 us
  Pallas kernels  12.3 us (85%)
  local copies, waits for them, and re-layouts  1.29 us (9%)
  between operations  0.64 us (4%)
    pallas_call x1, Pallas kernels, body(): pl.pallas_call(functools.partial(kernel, tiles, evals), out_shape=jax.Sha...  12.3 us
    squeeze x1, local copies, waits for them, and re-layouts, body(): return (out[0], out[1], out[2])  1.29 us

profile of v2, /device:TPU:0, one launch (start us, length us, event | category | flops | bytes accessed | tf_op | source)
XLA Modules:
  0.0 14.3 jit_solution(16972176126728280883)
XLA Ops:
  0.6 12.3 %shard_map.85 = f32[3,8,128]{2,1,0:T(8,128)} custom-call(f32[6,8,128]{2,1,0:T(8,128)} %geom_in.1, f32[8,128]{1,0:T(8,128)} %eta_in.1, f32[8,128]{1,0:T(8,128)} %phi_in.1, f32[1,4,4,32]{3,2,1,0:T(4,128)} %src_in.1, s32[4,8]{1,0:T(4,128)} %glen_in.1, s32[4]{0:T(128)} %owner_in.1), custom_call_target="tpu_custom_call" | custom-call | tf_op jit(solution)/shard_map/pallas_call | solution.py:307
  13.0 1.3 %slice_bitcast_fusion = (f32[8,128]{1,0:T(8,128)}, f32[8,128]{1,0:T(8,128)}, f32[8,128]{1,0:T(8,128)}) fusion(f32[3,8,128]{2,1,0:T(8,128)} %shard_map.85), kind=kLoop, calls=%fused_computation | loop fusion | bytes 24576 | tf_op jit(solution)/shard_map/squeeze | solution.py:340

commit v3 on v2

--- a/solution.py
+++ b/solution.py
@@ -82,15 +82,14 @@
 
     barrier = pltpu.get_barrier_semaphore()
 
-    def greet(k, carry):
-        other = lax.rem(me + k, peers)
+    def greet(other, carry):
         pl.semaphore_signal(
             barrier, inc=1,
             device_id=(lax.div(other, evals), lax.rem(other, evals)), device_id_type=MESH,
         )
         return carry
 
-    lax.fori_loop(1, peers, greet, 0)
+    lax.fori_loop(me + 1, peers, greet, 0)
 
     for copy in loads[:3]:
         copy.wait()
@@ -130,35 +129,60 @@
         cols = jnp.where(lane == 16 + k, v, cols)
     cols_out[...] = cols
 
-    pl.semaphore_wait(barrier, peers - 1)
-
-    def send(k, carry):
-        other = lax.rem(me + k, peers)
+    has_up, has_down = ti > 0, ti < tiles - 1
+    has_left, has_right = ev > 0, ev < evals - 1
+
+    def send(other):
         pltpu.make_async_remote_copy(
-            src_ref=row_out.at[0], dst_ref=got.at[me], send_sem=send_src, recv_sem=recv_src,
+            src_ref=row_out.at[0], dst_ref=got.at[me], send_sem=send_src,
+            recv_sem=recv_src.at[me],
             device_id=(lax.div(other, evals), lax.rem(other, evals)), device_id_type=MESH,
         ).start()
-        return carry
-
-    lax.fori_loop(1, peers, send, 0)
+
     first = pl.ds(0, 8)
     plan = [
-        (rows_top, halo_rows.at[1], (up, ev)),
-        (rows_bot, halo_rows.at[0], (down, ev)),
-        (cols_out, halo_cols.at[1], (ti, left)),
-        (cols_out, halo_cols.at[0], (ti, right)),
-        (rows_top.at[first], halo_diag.at[3], (up, left)),
-        (rows_top.at[first], halo_diag.at[2], (up, right)),
-        (rows_bot.at[first], halo_diag.at[1], (down, left)),
-        (rows_bot.at[first], halo_diag.at[0], (down, right)),
+        (rows_top, halo_rows.at[1], (up, ev), has_up, has_down),
+        (cols_out, halo_cols.at[1], (ti, left), has_left, has_right),
+        (rows_top.at[first], halo_diag.at[3], (up, left), has_up & has_left, has_down & has_right),
+        (rows_top.at[first], halo_diag.at[2], (up, right), has_up & has_right, has_down & has_left),
+        (rows_bot, halo_rows.at[0], (down, ev), has_down, has_up),
+        (cols_out, halo_cols.at[0], (ti, right), has_right, has_left),
+        (rows_bot.at[first], halo_diag.at[1], (down, left), has_down & has_left, has_up & has_right),
+        (rows_bot.at[first], halo_diag.at[0], (down, right), has_down & has_right, has_up & has_left),
     ]
     copies = []
-    for k, (a, b, where) in enumerate(plan):
+    for k, (a, b, where, sends, takes) in enumerate(plan):
         copy = pltpu.make_async_remote_copy(
             src_ref=a, dst_ref=b, send_sem=send_halo.at[k], recv_sem=recv_halo.at[k],
             device_id=where, device_id_type=MESH)
-        copy.start()
-        copies.append(copy)
+        copies.append((copy, sends, takes))
+
+    def start(some):
+        for copy, sends, _ in some:
+            pl.when(sends)(copy.start)
+
+    def send_back(other, carry):
+        send(other)
+        return carry
+
+    def arrived(d):
+        pltpu.make_async_copy(got.at[d], got.at[d], recv_src.at[d]).wait()
+
+    def answer(d, carry):
+        arrived(d)
+        send(d)
+        return carry
+
+    def collect(d, carry):
+        arrived(d)
+        return carry
+
+    @pl.when(me > 0)
+    def _():
+        pl.semaphore_wait(barrier, me)
+
+    lax.fori_loop(0, me, send_back, 0)
+    start(copies[:4])
 
     for k, v in enumerate(target_features(g)):
         tfeat[0:height, k, :] = v
@@ -166,65 +190,11 @@
     for f, v in enumerate((e, p)):
         ext[f, 8:16, 0:lanes] = v
 
-    others = got.at[pl.ds(0, peers - 1)]
-    pltpu.make_async_copy(others, others, recv_src).wait()
-    pltpu.make_async_copy(others, others, send_src).wait()
-
-    table = got[:, 0, :]
-    if tiles > ROUNDS:
-        picked = []
-        for r in range(ROUNDS):
-            v = jnp.zeros((evals, 4 * width), F32)
-            for t in range(tiles):
-                v = jnp.where(owner[r] == t, table[t * evals:(t + 1) * evals], v)
-            picked.append(v)
-        table = jnp.concatenate(picked, axis=0)
-    chunks = table.shape[0] // 4
-    group = lax.div(lax.broadcasted_iota(jnp.int32, (chunks, 4 * width), 1), width)
-    parts = [table[b * chunks:(b + 1) * chunks] for b in range(4)]
-    s = []
-    for f in range(4):
-        v = parts[f]
-        for b in range(4):
-            if b != f:
-                v = jnp.where(group == b, pltpu.roll(parts[b], ((b - f) % 4) * width, 1), v)
-        s.append(v)
-    y, q = s[:3], s[3]
-    for k, v in enumerate(source_features(y, q)):
-        sfeat[:, k, :] = v
-    wide = 4 * width
-    feat = lax.broadcasted_iota(jnp.int32, (wide, FEATS), 1)
-
-    def turn(a, carry):
-        t = sfeat[a].T
-        lhs[a, 0:wide, :] = jnp.where(feat < HALF, t, 0.0).astype(BF16)
-        lhs[a, wide:, :] = jnp.where(feat >= HALF, t, 0.0).astype(BF16)
-        return carry
-
-    lax.fori_loop(0, chunks, turn, 0, unroll=min(chunks, 8))
-
-    def velocity(n):
-        rhs = jnp.concatenate([tfeat[2 * n], tfeat[2 * n + 1]], axis=1).astype(BF16)
-
-        def add(a, acc):
-            both = jnp.dot(lhs[a], rhs, preferred_element_type=F32)
-            dist2, numer = both[:wide], both[wide:]
-            r = lax.rsqrt(dist2)
-            term = (numer * r) * (r * r)
-            return acc + jnp.sum(term.reshape(wide // 8, 8, 2 * lanes), axis=0)
-
-        acc = lax.fori_loop(0, chunks, add, jnp.zeros((8, 2 * lanes), F32), unroll=min(chunks, 8))
-        return jnp.sum(acc, axis=0, keepdims=True)
-
-    for n in range(height // 2):
-        w = velocity(n)
-        ext[2, 8 + 2 * n:9 + 2 * n, 0:lanes] = w[:, :lanes]
-        ext[2, 9 + 2 * n:10 + 2 * n, 0:lanes] = w[:, lanes:]
-
-    has_up, has_down = ti > 0, ti < tiles - 1
-    has_left, has_right = ev > 0, ev < evals - 1
-    for copy in copies:
-        copy.wait()
+    near_end = jnp.minimum(me + evals + 2, peers)
+    lax.fori_loop(me + 1, near_end, answer, 0)
+    start(copies[4:])
+    for copy, _, takes in copies:
+        pl.when(takes)(copy.wait_recv)
 
     above, below = halo_rows[0], halo_rows[1]
     near = [jnp.concatenate([above[4 + f:5 + f], below[4 + f:5 + f]], axis=0) for f in range(6)]
@@ -254,24 +224,79 @@
         ext[f, 16:17, lanes:] = jnp.where(
             has_down, side([halo_diag[2, f:f + 1, end:]], [halo_diag[3, f:f + 1, 0:1]]), 0.0)
 
-    w = velocity(height // 2)
-    ext[2, 7:8, 0:lanes] = jnp.where(has_up, w[:, :lanes], 0.0)
-    ext[2, 16:17, 0:lanes] = jnp.where(has_down, w[:, lanes:], 0.0)
-
+    wide = 4 * width
+    chunks = evals // 4
+    group = lax.div(lax.broadcasted_iota(jnp.int32, (chunks, wide), 1), width)
+    feat = lax.broadcasted_iota(jnp.int32, (wide, FEATS), 1)
+    blocks = height // 2 + 1
+    accs = [jnp.zeros((8, 2 * lanes), F32) for _ in range(blocks)]
     total = [jnp.zeros((height, wide), F32) for _ in range(2)]
     sides = [[c[:, k:k + 1] for k in range(o, o + 6)] for c, o in ((cl, 20), (cr, 4))]
     sides = [[jnp.broadcast_to(v, (height, wide)) for v in one] for one in sides]
-    for a in range(chunks):
-        ya = [jnp.broadcast_to(v[a:a + 1], (height, wide)) for v in s]
-        for k, t in enumerate(sides):
-            d = [t[c] - ya[c] for c in range(3)]
-            r = lax.rsqrt(d[0] * d[0] + d[1] * d[1] + d[2] * d[2] + EPS2)
-            numer = t[3] * d[0] + t[4] * d[1] + t[5] * d[2]
-            total[k] = total[k] + (ya[3] * numer * r) * (r * r)
+
+    def fetch(lo, hi):
+        lax.fori_loop(jnp.maximum(near_end, lo), jnp.maximum(near_end, hi), answer, 0)
+        lax.fori_loop(jnp.minimum(me, lo), jnp.minimum(me, hi), collect, 0)
+
+    if tiles > ROUNDS:
+        fetch(0, peers)
+    for step in range(ROUNDS):
+        if tiles > ROUNDS:
+            table = jnp.zeros((evals, wide), F32)
+            for t in range(tiles):
+                table = jnp.where(owner[step] == t, got[t * evals:(t + 1) * evals, 0, :], table)
+        else:
+            fetch(step * evals, (step + 1) * evals)
+            table = got[step * evals:(step + 1) * evals, 0, :]
+        parts = [table[b * chunks:(b + 1) * chunks] for b in range(4)]
+        s = []
+        for f in range(4):
+            v = parts[f]
+            for b in range(4):
+                if b != f:
+                    v = jnp.where(group == b, pltpu.roll(parts[b], ((b - f) % 4) * width, 1), v)
+            s.append(v)
+        for k, v in enumerate(source_features(s[:3], s[3])):
+            sfeat[step, :, k, :] = v
+        for a in range(chunks):
+            t = sfeat[step, a].T
+            lhs[step, a, 0:wide, :] = jnp.where(feat < HALF, t, 0.0).astype(BF16)
+            lhs[step, a, wide:, :] = jnp.where(feat >= HALF, t, 0.0).astype(BF16)
+
+        for n in range(blocks):
+            rhs = jnp.concatenate([tfeat[2 * n], tfeat[2 * n + 1]], axis=1).astype(BF16)
+            for a in range(chunks):
+                both = jnp.dot(lhs[step, a], rhs, preferred_element_type=F32)
+                dist2, numer = both[:wide], both[wide:]
+                r = lax.rsqrt(dist2)
+                term = (numer * r) * (r * r)
+                accs[n] = accs[n] + jnp.sum(term.reshape(wide // 8, 8, 2 * lanes), axis=0)
+
+        for a in range(chunks):
+            ya = [jnp.broadcast_to(v[a:a + 1], (height, wide)) for v in s]
+            for k, t in enumerate(sides):
+                d = [t[c] - ya[c] for c in range(3)]
+                r = lax.rsqrt(d[0] * d[0] + d[1] * d[1] + d[2] * d[2] + EPS2)
+                numer = t[3] * d[0] + t[4] * d[1] + t[5] * d[2]
+                total[k] = total[k] + (ya[3] * numer * r) * (r * r)
+
+    for n in range(blocks):
+        w = jnp.sum(accs[n], axis=0, keepdims=True)
+        if n < height // 2:
+            ext[2, 8 + 2 * n:9 + 2 * n, 0:lanes] = w[:, :lanes]
+            ext[2, 9 + 2 * n:10 + 2 * n, 0:lanes] = w[:, lanes:]
+        else:
+            ext[2, 7:8, 0:lanes] = jnp.where(has_up, w[:, :lanes], 0.0)
+            ext[2, 16:17, 0:lanes] = jnp.where(has_down, w[:, lanes:], 0.0)
     wl = jnp.sum(total[0], axis=1, keepdims=True)
     wr = jnp.sum(total[1], axis=1, keepdims=True)
     halo = jnp.where((lane == 0) & has_right, wr, 0.0)
     ext[2, 8:16, lanes:] = jnp.where((lane == end) & has_left, wl, halo)
+
+    others = got.at[pl.ds(0, peers - 1)]
+    pltpu.make_async_copy(others, others, send_src).wait()
+    for copy, sends, _ in copies:
+        pl.when(sends)(copy.wait_send)
 
     span = (24, 2 * lanes)
     ee, pp, ww = ext[0], ext[1], ext[2]
@@ -301,7 +326,7 @@
 def body(tiles, evals, target_geom, eta, phi, sources, group_len, owner):
     height, lanes = eta.shape
     width = sources.shape[3]
-    chunks = ROUNDS * evals // 4
+    chunks = evals // 4
     vmem = pl.BlockSpec(memory_space=pltpu.VMEM)
     hbm = pl.BlockSpec(memory_space=pltpu.HBM)
     out = pl.pallas_call(
@@ -325,12 +350,12 @@
             pltpu.VMEM((4, 8, lanes), F32),
             pltpu.VMEM((2, height, lanes), F32),
             pltpu.VMEM((height + 2, FEATS, lanes), F32),
-            pltpu.VMEM((chunks, FEATS, 4 * width), F32),
-            pltpu.VMEM((chunks, 8 * width, FEATS), BF16),
+            pltpu.VMEM((ROUNDS, chunks, FEATS, 4 * width), F32),
+            pltpu.VMEM((ROUNDS, chunks, 8 * width, FEATS), BF16),
             pltpu.VMEM((3, 24, 2 * lanes), F32),
             pltpu.SemaphoreType.DMA((6,)),
             pltpu.SemaphoreType.DMA,
-            pltpu.SemaphoreType.DMA,
+            pltpu.SemaphoreType.DMA((tiles * evals,)),
             pltpu.SemaphoreType.DMA((8,)),
             pltpu.SemaphoreType.DMA((8,)),
         ],

time: 14.5 us -> 21.8 us (1.50)
  the two profiles are of different devices: /device:TPU:0 before, /device:TPU:29 now
where the time goes in v3:
time: 21.8 us; the launch traced here: 21.6 us
  Pallas kernels  19.7 us (90%)
  local copies, waits for them, and re-layouts  1.29 us (6%)
  between operations  0.64 us (3%)
    pallas_call x1, Pallas kernels, body(): pl.pallas_call(functools.partial(kernel, tiles, evals), out_shape=jax.Sha...  19.7 us
    squeeze x1, local copies, waits for them, and re-layouts, body(): return (out[0], out[1], out[2])  1.29 us

profile of v3, /device:TPU:29, one launch (start us, length us, event | category | flops | bytes accessed | tf_op | source)
XLA Modules:
  0.0 21.6 jit_solution(3433660030880368879)
XLA Ops:
  0.6 19.7 %shard_map.85 = f32[3,8,128]{2,1,0:T(8,128)} custom-call(f32[6,8,128]{2,1,0:T(8,128)} %geom_in.1, f32[8,128]{1,0:T(8,128)} %eta_in.1, f32[8,128]{1,0:T(8,128)} %phi_in.1, f32[1,4,4,32]{3,2,1,0:T(4,128)} %src_in.1, s32[4,8]{1,0:T(4,128)} %glen_in.1, s32[4]{0:T(128)} %owner_in.1), custom_call_target="tpu_custom_call" | custom-call | tf_op jit(solution)/shard_map/pallas_call | solution.py:332
  20.3 1.3 %slice_bitcast_fusion = (f32[8,128]{1,0:T(8,128)}, f32[8,128]{1,0:T(8,128)}, f32[8,128]{1,0:T(8,128)}) fusion(f32[3,8,128]{2,1,0:T(8,128)} %shard_map.85), kind=kLoop, calls=%fused_computation | loop fusion | bytes 24576 | tf_op jit(solution)/shard_map/squeeze | solution.py:365

commit v4 on v2

--- a/solution.py
+++ b/solution.py
@@ -142,23 +142,27 @@
 
     lax.fori_loop(1, peers, send, 0)
     first = pl.ds(0, 8)
+    has_up, has_down = ti > 0, ti < tiles - 1
+    has_left, has_right = ev > 0, ev < evals - 1
     plan = [
-        (rows_top, halo_rows.at[1], (up, ev)),
-        (rows_bot, halo_rows.at[0], (down, ev)),
-        (cols_out, halo_cols.at[1], (ti, left)),
-        (cols_out, halo_cols.at[0], (ti, right)),
-        (rows_top.at[first], halo_diag.at[3], (up, left)),
-        (rows_top.at[first], halo_diag.at[2], (up, right)),
-        (rows_bot.at[first], halo_diag.at[1], (down, left)),
-        (rows_bot.at[first], halo_diag.at[0], (down, right)),
+        (rows_top, halo_rows.at[1], (up, ev), has_up, has_down),
+        (cols_out, halo_cols.at[1], (ti, left), has_left, has_right),
+        (rows_top.at[first], halo_diag.at[3], (up, left), has_up & has_left, has_down & has_right),
+        (rows_top.at[first], halo_diag.at[2], (up, right), has_up & has_right, has_down & has_left),
+        (rows_bot, halo_rows.at[0], (down, ev), has_down, has_up),
+        (cols_out, halo_cols.at[0], (ti, right), has_right, has_left),
+        (rows_bot.at[first], halo_diag.at[1], (down, left), has_down & has_left, has_up & has_right),
+        (rows_bot.at[first], halo_diag.at[0], (down, right), has_down & has_right, has_up & has_left),
     ]
     copies = []
-    for k, (a, b, where) in enumerate(plan):
+    for k, (a, b, where, sends, takes) in enumerate(plan):
         copy = pltpu.make_async_remote_copy(
             src_ref=a, dst_ref=b, send_sem=send_halo.at[k], recv_sem=recv_halo.at[k],
             device_id=where, device_id_type=MESH)
-        copy.start()
-        copies.append(copy)
+        copies.append((copy, sends, takes))
+
+    for copy, sends, _ in copies:
+        pl.when(sends)(copy.start)
 
     for k, v in enumerate(target_features(g)):
         tfeat[0:height, k, :] = v
@@ -221,10 +225,9 @@
         ext[2, 8 + 2 * n:9 + 2 * n, 0:lanes] = w[:, :lanes]
         ext[2, 9 + 2 * n:10 + 2 * n, 0:lanes] = w[:, lanes:]
 
-    has_up, has_down = ti > 0, ti < tiles - 1
-    has_left, has_right = ev > 0, ev < evals - 1
-    for copy in copies:
-        copy.wait()
+    for copy, sends, takes in copies:
+        pl.when(sends)(copy.wait_send)
+        pl.when(takes)(copy.wait_recv)
 
     above, below = halo_rows[0], halo_rows[1]
     near = [jnp.concatenate([above[4 + f:5 + f], below[4 + f:5 + f]], axis=0) for f in range(6)]

time: 14.5 us -> 14.5 us (level)
  no operation moved by 1% of the time
where the time goes in v4:
time: 14.5 us; the launch traced here: 14.3 us
  Pallas kernels  12.3 us (85%)
  local copies, waits for them, and re-layouts  1.29 us (9%)
  between operations  0.64 us (4%)
    pallas_call x1, Pallas kernels, body(): pl.pallas_call(functools.partial(kernel, tiles, evals), out_shape=jax.Sha...  12.3 us
    squeeze x1, local copies, waits for them, and re-layouts, body(): return (out[0], out[1], out[2])  1.29 us

profile of v4, /device:TPU:0, one launch (start us, length us, event | category | flops | bytes accessed | tf_op | source)
XLA Modules:
  0.0 14.3 jit_solution(1898372264376539973)
XLA Ops:
  0.6 12.3 %shard_map.85 = f32[3,8,128]{2,1,0:T(8,128)} custom-call(f32[6,8,128]{2,1,0:T(8,128)} %geom_in.1, f32[8,128]{1,0:T(8,128)} %eta_in.1, f32[8,128]{1,0:T(8,128)} %phi_in.1, f32[1,4,4,32]{3,2,1,0:T(4,128)} %src_in.1, s32[4,8]{1,0:T(4,128)} %glen_in.1, s32[4]{0:T(128)} %owner_in.1), custom_call_target="tpu_custom_call" | custom-call | tf_op jit(solution)/shard_map/pallas_call | solution.py:310
  13.0 1.3 %slice_bitcast_fusion = (f32[8,128]{1,0:T(8,128)}, f32[8,128]{1,0:T(8,128)}, f32[8,128]{1,0:T(8,128)}) fusion(f32[3,8,128]{2,1,0:T(8,128)} %shard_map.85), kind=kLoop, calls=%fused_computation | loop fusion | bytes 24576 | tf_op jit(solution)/shard_map/squeeze | solution.py:343
